TPU v7x, 512 devices: a whole 4x4x16 slice. The times are simulated.
512 devices in a mesh: seq: 128 (over z, y, core), head: 4 (over x).
Axes of the slice: x: 4, y: 4, z: 16, core: 2. Of those that a mesh axis runs over, the one named last changes fastest.
Arguments:
- patches: bfloat16 [32768, 1280], P('seq'), may hold values from -6 to 6
- norm_gain: float32 [1280], replicated, may hold values from 0.5 to 1.5
- w_qkv: bfloat16 [1280, 3, 1280], P('seq', None, 'head'), as said below
- w_out: bfloat16 [1280, 1280], P('head', 'seq'), may hold values from -0.15625 to 0.15625
- window_order: int32 [128, 64], P('seq'), may hold values from 0 to 63, each once within a row
- merge_gain: float32 [1280], replicated, may hold values from 0.5 to 1.5
- w_kv: bfloat16 [5120, 2, 1024], P('seq', None, 'head'), as said below
- queries: bfloat16 [256, 8192], P('seq', 'head'), may hold values from -6 to 6
- suffix_kv: bfloat16 [256, 64, 2, 1024], P('seq', None, None, 'head'), may hold values from -12 to 12
- question_lengths: int32 [256], P('seq'), may hold values from 1 to 64
- frame_range: int32 [256, 2], replicated, may hold values from 0 to 128, as said below
Outputs:
- answers: bfloat16 [256, 8192], P('seq', 'head')
Inputs may be any that keep to these rules, and one draw needn't show every extreme that they name: `window_order`: each row is an ordering of a frame's units; positions w * 16 to (w + 1) * 16 - 1 form window w. `frame_range`: the first entry of a row is below the second. `w_qkv`: entries of order one over the square root of 1280. `w_kv`: entries of order one over the square root of 5120.
All inputs are finite; a program needn't handle non-finite values.
Results may differ from a plain program's by a relative error of at most 0.007.
Values may be sent and summed in bfloat16 or wider, within the bound.
No kernel may reach another device: no remote copies, remote signals or barrier semaphores. Data moves between devices by JAX's collectives and lax.ppermute only.
A program may use at most 64 MiB of HBM per device.

v0:
```python
import jax
import jax.numpy as jnp
from jax import lax
from jax.sharding import Mesh
from jax.sharding import PartitionSpec as P

VD = 1280
VH = 16
HD = 128
FPATCH = 256
WIN = 64
SEQ = ("seq_0", "seq_1", "seq_2")
NEGATIVE = -1e30


def in_order(blocks, dim):
    dims = list(blocks.shape[1:])
    dims[dim] *= blocks.shape[0]
    return jnp.moveaxis(blocks, 0, dim).reshape(dims)


def all_blocks(value, axes, sequence):
    blocks = value[None]
    for k in sequence:
        blocks = lax.all_gather(blocks, axes[k], axis=0, tiled=True)
    current = [lax.axis_size(axes[k]) for k in reversed(sequence)]
    blocks = blocks.reshape(*current, *value.shape)
    turned = sorted(range(len(sequence)), key=lambda place: sequence[len(sequence) - 1 - place])
    return blocks.transpose(*turned, *range(len(sequence), blocks.ndim)).reshape(-1, *value.shape)


def whole_of(value, axes, sequence, dim):
    return in_order(all_blocks(value, axes, sequence), dim)


def from_everyone(value, axis):
    copies = jnp.broadcast_to(value, (lax.axis_size(axis), *value.shape))
    return lax.all_to_all(copies, axis, split_axis=0, concat_axis=0, tiled=True)


def of_everyone(value, axis):
    everything = from_everyone(value, axis)
    return jnp.sum(everything.astype(jnp.float32), axis=0)


def rms_scale(values, gain):
    return values * lax.rsqrt(jnp.mean(values * values, axis=-1, keepdims=True) + 1e-06) * gain


def frame_window(frame_rows, unit_order, local_heads, head_size):
    unit_count = unit_order.shape[0]
    grouped = frame_rows.reshape(unit_count, 4, 3, local_heads * head_size)[unit_order]
    windows = grouped.reshape(-1, WIN, 3, local_heads, head_size)
    scores = jnp.einsum(
        "wqhd,wkhd->whqk", windows[:, :, 0], windows[:, :, 1], preferred_element_type=jnp.float32
    ) * head_size ** (-0.5)
    weights = jax.nn.softmax(scores, axis=-1).astype(jnp.bfloat16)
    mixed = jnp.einsum(
        "whqk,wkhd->wqhd", weights, windows[:, :, 2], preferred_element_type=jnp.float32
    ).astype(jnp.bfloat16)
    mixed = mixed.reshape(unit_count, 4, local_heads * head_size)
    return (
        jnp.zeros_like(mixed)
        .at[unit_order]
        .set(mixed)
        .reshape(unit_count * 4, local_heads * head_size)
    )


def prefix_scores(asking, keys_values, bounds, frame_tokens):
    token_count = keys_values.shape[0]
    kv_local, head_size = (asking.shape[1], asking.shape[3])
    keys = keys_values[:, 0].reshape(token_count, kv_local, head_size)
    values = keys_values[:, 1].reshape(token_count, kv_local, head_size)
    frame_index = jnp.arange(token_count) // frame_tokens
    live = (frame_index[None, :] >= bounds[:, 0:1]) & (frame_index[None, :] < bounds[:, 1:2])
    scores = jnp.einsum(
        "qgjd,ngd->qgjn", asking, keys, preferred_element_type=jnp.float32
    ) * head_size ** (-0.5)
    return (jnp.where(live[:, None, None, :], scores, -jnp.inf), values)


def add_suffix(maxima, totals, weighted, asking, suffix_kv, lengths):
    quest_count, span = (suffix_kv.shape[0], suffix_kv.shape[1])
    kv_local, head_size = (asking.shape[1], asking.shape[3])
    keys = suffix_kv[:, :, 0].reshape(quest_count, span, kv_local, head_size)
    values = suffix_kv[:, :, 1].reshape(quest_count, span, kv_local, head_size)
    scores = jnp.einsum(
        "qgjd,qsgd->qgjs", asking, keys, preferred_element_type=jnp.float32
    ) * head_size ** (-0.5)
    live = (jnp.arange(span)[None, :] < lengths[:, None])[:, None, None, :]
    scores = jnp.where(live, scores, -jnp.inf)
    highest = jnp.maximum(maxima, jnp.max(scores, axis=-1))
    weights = jnp.exp(scores - highest[..., None])
    carried = jnp.exp(maxima - highest)
    totals = totals * carried + jnp.sum(weights, axis=-1)
    weighted = weighted * carried[..., None] + jnp.einsum(
        "qgjs,qsgd->qgjd", weights.astype(jnp.bfloat16), values, preferred_element_type=jnp.float32
    )
    return (weighted / totals[..., None]).reshape(quest_count, -1).astype(jnp.bfloat16)


def on_device(
    patches,
    norm_gain,
    w_qkv,
    w_out,
    window_order,
    merge_gain,
    w_kv,
    queries,
    suffix_kv,
    question_lengths,
    frame_range,
):
    row_count = patches.shape[0]
    columns = w_qkv.shape[2]
    head_size = VD // VH
    local_heads = columns // head_size
    source = patches.astype(jnp.float32)
    normed = rms_scale(source, norm_gain).astype(jnp.bfloat16)
    portion = whole_of(w_qkv, SEQ, (1, 0, 2), 0)
    inputs = normed
    projected = jnp.dot(
        inputs, portion.reshape(portion.shape[0], 3 * columns), preferred_element_type=jnp.float32
    )
    projected = projected.astype(jnp.bfloat16).reshape(window_order.shape[0], -1, 3, columns)
    attended = jax.vmap(
        lambda frame_rows, unit_order: frame_window(frame_rows, unit_order, local_heads, head_size)
    )(projected, window_order)
    attended = attended.reshape(row_count, columns)
    w_full = lax.all_gather(w_out, SEQ, axis=1, tiled=True)
    summed = of_everyone(
        jnp.dot(attended, w_full, preferred_element_type=jnp.float32).astype(jnp.bfloat16), "head"
    ).astype(jnp.float32)
    merged_all = (
        rms_scale(source + summed, merge_gain).astype(jnp.bfloat16).reshape(row_count // 4, 4 * VD)
    )
    token_count = merged_all.shape[0]
    kv_columns = w_kv.shape[2]
    portion = lax.all_gather(w_kv, SEQ, axis=0, tiled=True)
    inputs = merged_all
    visual = jnp.dot(
        inputs,
        portion.reshape(portion.shape[0], 2 * kv_columns),
        preferred_element_type=jnp.float32,
    )
    visual = visual.astype(jnp.bfloat16).reshape(token_count, 2, kv_columns)
    quest_count = queries.shape[0]
    kv_local = kv_columns // HD
    asking = queries.reshape(quest_count, kv_local, -1, HD)
    group = asking.shape[2]
    frame_tokens = FPATCH // 4
    seq_index = lax.axis_index(SEQ)
    own_bounds = lax.dynamic_slice_in_dim(frame_range, seq_index * quest_count, quest_count, 0)
    maxima = jnp.full((quest_count, kv_local, group), NEGATIVE, jnp.float32)
    scores, values = prefix_scores(
        asking, whole_of(visual, SEQ, (1, 0, 2), 0), own_bounds, frame_tokens
    )
    highest = jnp.maximum(maxima, jnp.max(scores, axis=-1))
    weights = jnp.exp(scores - highest[..., None])
    totals = jnp.sum(weights, axis=-1)
    weighted = jnp.einsum(
        "qgjn,ngd->qgjd", weights.astype(jnp.bfloat16), values, preferred_element_type=jnp.float32
    )
    maxima, totals, weighted = (highest, totals, weighted)
    return add_suffix(maxima, totals, weighted, asking, suffix_kv, question_lengths)


def solution(mesh):
    torus = Mesh(
        mesh.devices.reshape(16, 4, 2, mesh.shape["head"]), ("seq_0", "seq_1", "seq_2", "head")
    )
    in_specs = (
        P(SEQ, None),
        P(),
        P(SEQ, None, "head"),
        P("head", SEQ),
        P(SEQ, None),
        P(),
        P(SEQ, None, "head"),
        P(SEQ, "head"),
        P(SEQ, None, None, "head"),
        P(SEQ),
        P(),
    )
    out_specs = P(SEQ, "head")
    return jax.shard_map(
        on_device, mesh=torus, in_specs=in_specs, out_specs=out_specs, check_vma=False
    )
```

profile of v0, /device:TPU:1, one launch (start us, length us, event | category | flops | bytes accessed | tf_op | source)
XLA Modules:
  0.0 429.4 jit_solution(2125874026757927389)
XLA Ops:
  6.5 12.5 %all-gather = bf16[40,3,320]{2,1,0:T(4,128)(2,1)} all-gather(bf16[10,3,320]{2,1,0:T(4,128)(2,1)} %param.13), channel_id=2, replica_groups=mesh['seq_0'=16,'seq_1'=4,'seq_2'=2,'head'=4] {'seq_1'}, dimensions={0}, use_global_device_ids=true | all-gather | bytes 96000 | tf_op jit(solution)/shard_map/all_gather | solution.py:25
  19.1 69.1 %all-gather.8.cloned.1.call-done = bf16[64,10,3,320]{3,2,1,0:T(4,128)(2,1)} async-done(((bf16[4,10,3,320]{3,2,1,0:T(4,128)(2,1)}), bf16[64,10,3,320]{3,2,1,0:T(4,128)(2,1)}) %all-gather.8.cloned.1.call-update) | async-done | bytes 1228816 | tf_op jit(solution)/shard_map/all_gather | solution.py:25
  88.2 3.1 copy.104
  92.1 111.3 %all-gather.1 = bf16[128,10,320]{2,1,0:T(8,128)(2,1)S(1)} all-gather(bf16[1,10,320]{2,1,0:T(8,128)(2,1)S(1)} %bitcast.119), channel_id=1, replica_groups=mesh['seq_0'=16,'seq_1'=4,'seq_2'=2,'head'=4] {'seq_0','seq_1','seq_2'}, dimensions={0}, use_global_device_ids=true | all-gather | bytes 825600 | tf_op jit(solution)/shard_map/all_gather | solution.py:132
  203.4 1.5 reshape.215
  205.2 4.6 %reshape.179 = bf16[2,16,4,10,3,320]{5,2,1,0,4,3:T(4,128)(2,1)S(1)} reshape(bf16[128,10,3,320]{3,0,2,1:T(8,128)(2,1)} %all-gather.10.cloned.1.call-done) | data formatting | bytes 4915200 | tf_op jit(solution)/shard_map/reshape | solution.py:27
  209.8 4.5 %copy.105 = bf16[16,4,2,10,3,320]{5,4,3,2,1,0:T(4,128)(2,1)} copy(bf16[16,4,2,10,3,320]{5,1,0,2,4,3:T(4,128)(2,1)S(1)} %bitcast.112) | data formatting | bytes 4915200 | tf_op jit(solution)/shard_map/transpose | solution.py:29
  214.3 7.0 %reshape_reshape_reshape.3 = bf16[1280,960]{1,0:T(8,128)(2,1)S(1)} reshape(bf16[16,4,2,10,3,320]{5,4,3,2,1,0:T(4,128)(2,1)} %copy.105) | data formatting | bytes 4915200 | tf_op jit(solution)/shard_map/reshape;reshape;reshape | solution.py:125
  221.3 2.0 convolution_convert_fusion.1
  223.3 1.2 copy.106
  225.2 1.1 gather_fusion
  228.9 2.5 scatter_fusion
  232.2 35.4 %all_to_all.5 = bf16[4,256,1280]{2,1,0:T(8,128)(2,1)S(1)} all-to-all(bf16[4,256,1280]{2,1,0:T(8,128)(2,1)S(1)} %broadcast_in_dim.37), channel_id=1, replica_groups=mesh['seq_0'=16,'seq_1'=4,'seq_2'=2,'head'=4] {'head'}, dimensions={0} | all-to-all | bytes 5242880 | tf_op jit(solution)/shard_map/all_to_all | solution.py:38
  269.0 3.4 copy.144
  272.4 1.0 convolution_convert_fusion.3
  273.5 11.1 %all_gather.29 = bf16[4,64,2,256]{3,1,2,0:T(8,128)(2,1)} all-gather(bf16[1,64,2,256]{3,1,2,0:T(8,128)(2,1)S(1)} %copy.114), channel_id=1, replica_groups=mesh['seq_0'=16,'seq_1'=4,'seq_2'=2,'head'=4] {'seq_1'}, dimensions={0}, use_global_device_ids=true | all-gather | bytes 327680 | tf_op jit(solution)/shard_map/all_gather | solution.py:25
  284.7 66.7 %all-gather.14.cloned.1.call-done = bf16[64,64,2,256]{3,1,2,0:T(8,128)(2,1)} async-done(((bf16[4,64,2,256]{3,1,2,0:T(8,128)(2,1)}), bf16[64,64,2,256]{3,1,2,0:T(8,128)(2,1)}) %all-gather.14.cloned.1.call-update) | async-done | bytes 4194320 | tf_op jit(solution)/shard_map/all_gather | solution.py:25
  352.5 38.0 %all-gather.16.cloned.1.call-done = bf16[128,64,2,256]{3,1,2,0:T(8,128)(2,1)} async-done(((bf16[64,64,2,256]{3,1,2,0:T(8,128)(2,1)}), bf16[128,64,2,256]{3,1,2,0:T(8,128)(2,1)}) %all-gather.16.cloned.1.call-update) | async-done | bytes 8388624 | tf_op jit(solution)/shard_map/all_gather | solution.py:25
  390.5 8.3 %copy.115 = bf16[16,4,2,64,2,256]{5,3,2,1,0,4:T(8,128)(2,1)} copy(bf16[16,4,2,64,2,256]{5,3,4,1,0,2:T(8,128)(2,1)} %bitcast.113) | data formatting | bytes 16777216 | tf_op jit(solution)/shard_map/transpose | solution.py:29
  398.7 5.7 %fusion.36 = (bf16[8192,1,256]{2,0,1:T(8,128)(2,1)}, bf16[8192,1,256]{2,0,1:T(8,128)(2,1)}) fusion(bf16[8192,2,256]{2,0,1:T(8,128)(2,1)} %bitcast.108), kind=kLoop, calls=%fused_computation.81 | loop fusion | bytes 16777216 | tf_op jit(solution)/shard_map/slice | solution.py:73
  404.4 6.4 %copy.116 = bf16[8192,1,256]{0,2,1:T(8,128)(2,1)} copy(bf16[8192,1,256]{2,0,1:T(8,128)(2,1)} %get-tuple-element.10) | data formatting | bytes 8388608 | tf_op jit(solution)/shard_map/slice | solution.py:74
  410.8 6.4 %copy.117 = bf16[8192,1,256]{0,2,1:T(8,128)(2,1)} copy(bf16[8192,1,256]{2,0,1:T(8,128)(2,1)} %get-tuple-element.9) | data formatting | bytes 8388608 | tf_op jit(solution)/shard_map/slice | solution.py:73
  417.2 3.1 fusion.40
  420.8 1.2 fusion.11
  (77 shorter events, 8.9 us)
Async XLA Ops:
  6.5 344.9 %copy-start = (s32[256,2]{0,1:T(2,128)S(1)}, s32[256,2]{0,1:T(2,128)}, u32[]{:S(2)}) copy-start(s32[256,2]{0,1:T(2,128)} %param.21) | copy-start | bytes 6148
  6.5 85.6 %copy-start.7 = (bf16[320,10]{0,1:T(8,128)(2,1)S(1)}, bf16[320,10]{0,1:T(8,128)(2,1)}, u32[]{:S(2)}) copy-start(bf16[320,10]{0,1:T(8,128)(2,1)} %param.14) | copy-start | bytes 19204
  6.5 81.7 %all-gather.8.cloned.1.call-start = ((), (), s32[]{:S(2)}) async-start(), calls=%async_computation.1 | async-start | bytes 2088960 | tf_op jit(solution)/shard_map/all_gather | solution.py:25
  19.1 186.1 %all-gather.10.cloned.1.call-start = ((), (), s32[]{:S(2)}) async-start(), calls=%async_computation.2 | async-start | bytes 4423680 | tf_op jit(solution)/shard_map/all_gather | solution.py:25
  91.3 113.6 %copy-start.10 = (s32[1,64]{1,0:T(1,128)S(1)}, s32[1,64]{1,0:T(1,128)}, u32[]{:S(2)}) copy-start(s32[1,64]{1,0:T(1,128)} %param.15) | copy-start | bytes 772
  91.3 113.6 %copy-start.2 = (bf16[256,1280]{1,0:T(8,128)(2,1)S(1)}, bf16[256,1280]{1,0:T(8,128)(2,1)}, u32[]{:S(2)}) copy-start(bf16[256,1280]{1,0:T(8,128)(2,1)} %param.11) | copy-start | bytes 1966084
  91.3 177.7 %all-gather.12.cloned.1.call-start = ((), (), s32[]{:S(2)}) async-start(), calls=%async_computation.3 | async-start | bytes 5283840 | tf_op jit(solution)/shard_map/all_gather | solution.py:141
  92.1 259.3 %all-gather.14.cloned.1.call-start = ((), (), s32[]{:S(2)}) async-start(), calls=%async_computation.4 | async-start | bytes 4456448 | tf_op jit(solution)/shard_map/all_gather | solution.py:25
  214.3 7.0 %copy-start.3 = (bf16[256,1280]{1,0:T(8,128)(2,1)S(1)}, bf16[256,1280]{1,0:T(8,128)(2,1)}, u32[]{:S(2)}) copy-start(bf16[256,1280]{1,0:T(8,128)(2,1)} %param.11) | copy-start | bytes 1966084
  214.3 7.0 %copy-start.9 = (f32[1280]{0:T(1024)S(1)}, f32[1280]{0:T(1024)}, u32[]{:S(2)}) copy-start(f32[1280]{0:T(1024)} %param.12) | copy-start | bytes 15364
  227.8 3.7 copy-start.4
  267.6 0.7 copy-start.8
  273.4 78.1 %copy-start.5 = (bf16[2,64,2,256]{3,2,1,0:T(2,128)(2,1)S(1)}, bf16[2,64,2,256]{3,2,1,0:T(2,128)(2,1)}, u32[]{:S(2)}) copy-start(bf16[2,64,2,256]{3,2,1,0:T(2,128)(2,1)} %param.19) | copy-start | bytes 393220
  273.5 78.5 %copy-start.11 = (s32[2]{0:T(128)S(1)}, s32[2]{0:T(128)}, u32[]{:S(2)}) copy-start(s32[2]{0:T(128)} %param.20) | copy-start | bytes 28
  273.5 78.6 %copy-start.6 = (bf16[2,2048]{1,0:T(2,128)(2,1)S(1)}, bf16[2,2048]{1,0:T(2,128)(2,1)}, u32[]{:S(2)}) copy-start(bf16[2,2048]{1,0:T(2,128)(2,1)} %param.18) | copy-start | bytes 24580
  284.6 105.8 %all-gather.16.cloned.1.call-start = ((), (), s32[]{:S(2)}) async-start(), calls=%async_computation.5 | async-start | bytes 12582912 | tf_op jit(solution)/shard_map/all_gather | solution.py:25
  417.2 3.6 copy-start.1
Sparse Core Ops, SparseCore 0:
  19.2 68.9 all-gather.7
  91.4 30.2 all-gather.9
  124.9 143.7 all-gather.11
  284.8 66.5 all-gather.13
  353.3 37.1 all-gather.15
where the time goes:
time: 430 us; the launch traced here: 429 us
  waiting for transfers between devices  175 us (41%)
  blocking collectives  170 us (40%)
  local copies, waits for them, and re-layouts  59.8 us (14%)
  between operations  13.5 us (3%)
  matrix products  9.15 us (2%)
    all_gather x4, waiting for transfers between devices, all_blocks(): blocks = lax.all_gather(blocks, axes[k], axis=0, tiled=True)  174 us
    all_gather x1, blocking collectives, on_device(): w_full = lax.all_gather(w_out, SEQ, axis=1, tiled=True)  111 us
    all_to_all x1, blocking collectives, from_everyone(): return lax.all_to_all(copies, axis, split_axis=0, concat_axis=0, tiled=True)  35.4 us
    all_gather x2, blocking collectives, all_blocks(): blocks = lax.all_gather(blocks, axes[k], axis=0, tiled=True)  23.6 us
    transpose x2, local copies, waits for them, and re-layouts, all_blocks(): blocks.transpose(*turned, *range(len(sequence), blocks.ndim))  12.7 us
    slice x2, local copies, waits for them, and re-layouts, prefix_scores(): keys = keys_values[:, 0].reshape(token_count, kv_local, head_size)  12.1 us
  transfers between devices with their start and end apart: 5, of which 3 were waited for; matrix products, arithmetic and copies ran while one was open for 7% of the time, Pallas kernels for 0%

commit v1 on v0

--- a/solution.py
+++ b/solution.py
@@ -129,7 +129,9 @@
         lambda frame_rows, unit_order: frame_window(frame_rows, unit_order, local_heads, head_size)
     )(projected, window_order)
     attended = attended.reshape(row_count, columns)
-    w_full = lax.all_gather(w_out, SEQ, axis=1, tiled=True)
+    w_full = jnp.concatenate(
+        lax.all_to_all(jnp.stack([w_out] * lax.axis_size(SEQ)), SEQ, 0, 0), axis=1
+    )
     summed = of_everyone(
         jnp.dot(attended, w_full, preferred_element_type=jnp.float32).astype(jnp.bfloat16), "head"
     ).astype(jnp.float32)

time: 430 us -> 437 us (1.016)
  blocking collectives: 170 us -> 55 us
  waiting for transfers between devices: 175 us -> 274 us
  starting transfers between devices: 0.17 us -> 22.1 us
    all_gather x1 -> x0, blocking collectives: 111 us -> none  [on_device(): w_full = lax.all_gather(w_out, SEQ, axis=1, tiled=True)]
    all_to_all x0 -> x1, waiting for transfers between devices: none -> 75.3 us  [on_device(): lax.all_to_all(jnp.stack([w_out] * lax.axis_size(SEQ)), SEQ, 0, 0)]
    all_gather x1, waiting for transfers between devices: 0.02 us -> 23 us  [on_device(): portion = lax.all_gather(w_kv, SEQ, axis=0, tiled=True)]
    all_to_all x0 -> x1, starting transfers between devices: none -> 21.7 us  [on_device(): lax.all_to_all(jnp.stack([w_out] * lax.axis_size(SEQ)), SEQ, 0, 0)]
  transfers between devices with their start and end apart: 5 -> 6, of which waited for: 3 -> 5; matrix products, arithmetic and copies ran while one was open for 7% -> 7% of each run, Pallas kernels for 0% -> 0%
where the time goes in v1:
time: 437 us; the launch traced here: 436 us
  waiting for transfers between devices  274 us (63%)
  local copies, waits for them, and re-layouts  60.8 us (14%)
  blocking collectives  55 us (13%)
  starting transfers between devices  22.1 us (5%)
  between operations  13.5 us (3%)
  matrix products  9.17 us (2%)
    all_gather x4, waiting for transfers between devices, all_blocks(): blocks = lax.all_gather(blocks, axes[k], axis=0, tiled=True)  175 us
    all_to_all x1, waiting for transfers between devices, on_device(): lax.all_to_all(jnp.stack([w_out] * lax.axis_size(SEQ)), SEQ, 0, 0)  75.3 us
    all_to_all x1, blocking collectives, from_everyone(): return lax.all_to_all(copies, axis, split_axis=0, concat_axis=0, tiled=True)  32.2 us
    all_gather x1, waiting for transfers between devices, on_device(): portion = lax.all_gather(w_kv, SEQ, axis=0, tiled=True)  23 us
    all_gather x2, blocking collectives, all_blocks(): blocks = lax.all_gather(blocks, axes[k], axis=0, tiled=True)  22.8 us
    all_to_all x1, starting transfers between devices, on_device(): lax.all_to_all(jnp.stack([w_out] * lax.axis_size(SEQ)), SEQ, 0, 0)  21.7 us
    transpose x2, local copies, waits for them, and re-layouts, all_blocks(): blocks.transpose(*turned, *range(len(sequence), blocks.ndim))  12.7 us
    slice x2, local copies, waits for them, and re-layouts, prefix_scores(): keys = keys_values[:, 0].reshape(token_count, kv_local, head_size)  12.1 us
  transfers between devices with their start and end apart: 6, of which 5 were waited for; matrix products, arithmetic and copies ran while one was open for 7% of the time, Pallas kernels for 0%

profile of v1, /device:TPU:1, one launch (start us, length us, event | category | flops | bytes accessed | tf_op | source)
XLA Modules:
  0.0 436.4 jit_solution(7356428745116236303)
XLA Ops:
  6.5 12.5 %all-gather = bf16[40,3,320]{2,1,0:T(4,128)(2,1)} all-gather(bf16[10,3,320]{2,1,0:T(4,128)(2,1)} %param.13), channel_id=2, replica_groups=mesh['seq_0'=16,'seq_1'=4,'seq_2'=2,'head'=4] {'seq_1'}, dimensions={0}, use_global_device_ids=true | all-gather | bytes 96000 | tf_op jit(solution)/shard_map/all_gather | solution.py:25
  19.1 69.1 %all-gather.7.cloned.1.call-done = bf16[64,10,3,320]{3,2,1,0:T(4,128)(2,1)} async-done(((bf16[4,10,3,320]{3,2,1,0:T(4,128)(2,1)}), bf16[64,10,3,320]{3,2,1,0:T(4,128)(2,1)}) %all-gather.7.cloned.1.call-update) | async-done | bytes 1228816 | tf_op jit(solution)/shard_map/all_gather | solution.py:25
  88.2 2.9 copy.105
  92.0 1.4 stack.2
  93.4 21.7 %all-to-all-start = ((bf16[128,320,10]{1,2,0:T(8,128)(2,1)}), bf16[128,320,10]{1,2,0:T(8,128)(2,1)S(1)}, u32[]{:S(2)}, u32[]{:S(2)}) async-start(bf16[128,320,10]{1,2,0:T(8,128)(2,1)} %stack.2), calls=%async_computation | async-start | bytes 3145728 | tf_op jit(solution)/shard_map/all_to_all | solution.py:133
  115.6 75.3 %all-to-all-done = bf16[128,320,10]{1,2,0:T(8,128)(2,1)S(1)} async-done(((bf16[128,320,10]{1,2,0:T(8,128)(2,1)}), bf16[128,320,10]{1,2,0:T(8,128)(2,1)S(1)}, u32[]{:S(2)}, u32[]{:S(2)}) %all-to-all-start) | async-done | bytes 819232 | tf_op jit(solution)/shard_map/all_to_all | solution.py:133
  190.9 1.4 reshape.195
  192.3 4.6 %reshape.187 = bf16[2,16,4,10,3,320]{5,2,1,0,4,3:T(4,128)(2,1)S(1)} reshape(bf16[128,10,3,320]{3,0,2,1:T(8,128)(2,1)} %all-gather.9.cloned.1.call-done) | data formatting | bytes 4915200 | tf_op jit(solution)/shard_map/reshape | solution.py:27
  197.0 4.5 %copy.106 = bf16[16,4,2,10,3,320]{5,4,3,2,1,0:T(4,128)(2,1)} copy(bf16[16,4,2,10,3,320]{5,1,0,2,4,3:T(4,128)(2,1)S(1)} %bitcast.112) | data formatting | bytes 4915200 | tf_op jit(solution)/shard_map/transpose | solution.py:29
  201.5 6.9 %reshape_reshape_reshape.3 = bf16[1280,960]{1,0:T(8,128)(2,1)S(1)} reshape(bf16[16,4,2,10,3,320]{5,4,3,2,1,0:T(4,128)(2,1)} %copy.106) | data formatting | bytes 4915200 | tf_op jit(solution)/shard_map/reshape;reshape;reshape | solution.py:125
  208.4 2.0 convolution_convert_fusion.1
  210.4 1.2 copy.107
  216.1 2.5 scatter_fusion
  219.3 32.2 %all_to_all.10 = bf16[4,256,1280]{2,1,0:T(8,128)(2,1)S(1)} all-to-all(bf16[4,256,1280]{2,1,0:T(8,128)(2,1)S(1)} %broadcast_in_dim.37), channel_id=1, replica_groups=mesh['seq_0'=16,'seq_1'=4,'seq_2'=2,'head'=4] {'head'}, dimensions={0} | all-to-all | bytes 5242880 | tf_op jit(solution)/shard_map/all_to_all | solution.py:38
  252.9 23.0 %all-gather.11.cloned.1.call-done = bf16[5120,2,256]{2,1,0:T(2,128)(2,1)} async-done(((bf16[40,2,256]{2,1,0:T(2,128)(2,1)}), bf16[5120,2,256]{2,1,0:T(2,128)(2,1)}) %all-gather.11.cloned.1.call-update) | async-done | bytes 5242896 | tf_op jit(solution)/shard_map/all_gather | solution.py:143
  275.9 3.4 copy.145
  280.4 10.2 %all_gather.25 = bf16[4,64,2,256]{3,1,2,0:T(8,128)(2,1)} all-gather(bf16[1,64,2,256]{3,1,2,0:T(8,128)(2,1)S(1)} %copy.115), channel_id=1, replica_groups=mesh['seq_0'=16,'seq_1'=4,'seq_2'=2,'head'=4] {'seq_1'}, dimensions={0}, use_global_device_ids=true | all-gather | bytes 327680 | tf_op jit(solution)/shard_map/all_gather | solution.py:25
  290.7 67.8 %all-gather.13.cloned.1.call-done = bf16[64,64,2,256]{3,1,2,0:T(8,128)(2,1)} async-done(((bf16[4,64,2,256]{3,1,2,0:T(8,128)(2,1)}), bf16[64,64,2,256]{3,1,2,0:T(8,128)(2,1)}) %all-gather.13.cloned.1.call-update) | async-done | bytes 4194320 | tf_op jit(solution)/shard_map/all_gather | solution.py:25
  359.6 38.0 %all-gather.15.cloned.1.call-done = bf16[128,64,2,256]{3,1,2,0:T(8,128)(2,1)} async-done(((bf16[64,64,2,256]{3,1,2,0:T(8,128)(2,1)}), bf16[128,64,2,256]{3,1,2,0:T(8,128)(2,1)}) %all-gather.15.cloned.1.call-update) | async-done | bytes 8388624 | tf_op jit(solution)/shard_map/all_gather | solution.py:25
  397.6 8.3 %copy.116 = bf16[16,4,2,64,2,256]{5,3,2,1,0,4:T(8,128)(2,1)} copy(bf16[16,4,2,64,2,256]{5,3,4,1,0,2:T(8,128)(2,1)} %bitcast.113) | data formatting | bytes 16777216 | tf_op jit(solution)/shard_map/transpose | solution.py:29
  405.8 5.7 %fusion.36 = (bf16[8192,1,256]{2,0,1:T(8,128)(2,1)}, bf16[8192,1,256]{2,0,1:T(8,128)(2,1)}) fusion(bf16[8192,2,256]{2,0,1:T(8,128)(2,1)} %bitcast.108), kind=kLoop, calls=%fused_computation.81 | loop fusion | bytes 16777216 | tf_op jit(solution)/shard_map/slice | solution.py:73
  411.5 6.3 %copy.117 = bf16[8192,1,256]{0,2,1:T(8,128)(2,1)} copy(bf16[8192,1,256]{2,0,1:T(8,128)(2,1)} %get-tuple-element.10) | data formatting | bytes 8388608 | tf_op jit(solution)/shard_map/slice | solution.py:74
  417.9 6.4 %copy.118 = bf16[8192,1,256]{0,2,1:T(8,128)(2,1)} copy(bf16[8192,1,256]{2,0,1:T(8,128)(2,1)} %get-tuple-element.9) | data formatting | bytes 8388608 | tf_op jit(solution)/shard_map/slice | solution.py:73
  424.2 3.1 fusion.40
  (79 shorter events, 12.4 us)
Async XLA Ops:
  6.5 352.0 %copy-start = (s32[256,2]{0,1:T(2,128)S(1)}, s32[256,2]{0,1:T(2,128)}, u32[]{:S(2)}) copy-start(s32[256,2]{0,1:T(2,128)} %param.21) | copy-start | bytes 6148
  6.5 85.4 %copy-start.7 = (bf16[320,10]{0,1:T(8,128)(2,1)S(1)}, bf16[320,10]{0,1:T(8,128)(2,1)}, u32[]{:S(2)}) copy-start(bf16[320,10]{0,1:T(8,128)(2,1)} %param.14) | copy-start | bytes 19204
  6.5 81.7 %all-gather.7.cloned.1.call-start = ((), (), s32[]{:S(2)}) async-start(), calls=%async_computation.2 | async-start | bytes 2088960 | tf_op jit(solution)/shard_map/all_gather | solution.py:25
  19.1 173.2 %all-gather.9.cloned.1.call-start = ((), (), s32[]{:S(2)}) async-start(), calls=%async_computation.3 | async-start | bytes 4423680 | tf_op jit(solution)/shard_map/all_gather | solution.py:25
  91.2 24.1 %copy-start.10 = (s32[1,64]{1,0:T(1,128)S(1)}, s32[1,64]{1,0:T(1,128)}, u32[]{:S(2)}) copy-start(s32[1,64]{1,0:T(1,128)} %param.15) | copy-start | bytes 772
  91.2 24.2 %copy-start.2 = (bf16[256,1280]{1,0:T(8,128)(2,1)S(1)}, bf16[256,1280]{1,0:T(8,128)(2,1)}, u32[]{:S(2)}) copy-start(bf16[256,1280]{1,0:T(8,128)(2,1)} %param.11) | copy-start | bytes 1966084
  91.2 184.7 %all-gather.11.cloned.1.call-start = ((), (), s32[]{:S(2)}) async-start(), calls=%async_computation.4 | async-start | bytes 5283840 | tf_op jit(solution)/shard_map/all_gather | solution.py:143
  93.4 97.6 %all-to-all-start = ((bf16[128,320,10]{1,2,0:T(8,128)(2,1)}), bf16[128,320,10]{1,2,0:T(8,128)(2,1)S(1)}, u32[]{:S(2)}, u32[]{:S(2)}) async-start(bf16[128,320,10]{1,2,0:T(8,128)(2,1)} %stack.2), calls=%async_computation | async-start | bytes 3145728 | tf_op jit(solution)/shard_map/all_to_all | solution.py:133
  115.1 243.4 %all-gather.13.cloned.1.call-start = ((), (), s32[]{:S(2)}) async-start(), calls=%async_computation.5 | async-start | bytes 4456448 | tf_op jit(solution)/shard_map/all_gather | solution.py:25
  201.4 6.9 %copy-start.3 = (bf16[256,1280]{1,0:T(8,128)(2,1)S(1)}, bf16[256,1280]{1,0:T(8,128)(2,1)}, u32[]{:S(2)}) copy-start(bf16[256,1280]{1,0:T(8,128)(2,1)} %param.11) | copy-start | bytes 1966084
  201.5 6.9 %copy-start.9 = (f32[1280]{0:T(1024)S(1)}, f32[1280]{0:T(1024)}, u32[]{:S(2)}) copy-start(f32[1280]{0:T(1024)} %param.12) | copy-start | bytes 15364
  214.9 3.7 copy-start.4
  251.5 0.7 copy-start.8
  280.3 78.3 %copy-start.5 = (bf16[2,64,2,256]{3,2,1,0:T(2,128)(2,1)S(1)}, bf16[2,64,2,256]{3,2,1,0:T(2,128)(2,1)}, u32[]{:S(2)}) copy-start(bf16[2,64,2,256]{3,2,1,0:T(2,128)(2,1)} %param.19) | copy-start | bytes 393220
  280.4 78.8 %copy-start.11 = (s32[2]{0:T(128)S(1)}, s32[2]{0:T(128)}, u32[]{:S(2)}) copy-start(s32[2]{0:T(128)} %param.20) | copy-start | bytes 28
  280.4 78.8 %copy-start.6 = (bf16[2,2048]{1,0:T(2,128)(2,1)S(1)}, bf16[2,2048]{1,0:T(2,128)(2,1)}, u32[]{:S(2)}) copy-start(bf16[2,2048]{1,0:T(2,128)(2,1)} %param.18) | copy-start | bytes 24580
  290.7 106.9 %all-gather.15.cloned.1.call-start = ((), (), s32[]{:S(2)}) async-start(), calls=%async_computation.6 | async-start | bytes 12582912 | tf_op jit(solution)/shard_map/all_gather | solution.py:25
  424.2 3.6 copy-start.1
Sparse Core Ops, SparseCore 0:
  19.2 68.9 all-gather.6
  91.3 30.2 all-gather.8
  124.8 151.1 all-gather.10
  290.8 67.6 all-gather.12
  360.4 37.1 all-gather.14
